TPU v7x, 32 devices: a whole 2x2x4 slice. The times are simulated.
32 devices in a mesh: groups: 2 (over y), band: 4 (over z), inner: 4 (over x, core).
Axes of the slice: x: 2, y: 2, z: 4, core: 2. Of those that a mesh axis runs over, the one named last changes fastest.
Arguments:
- grid_rows: bfloat16 [32768, 512], P(('groups', 'band', 'inner')), parts along dimension 0, may hold values from -6 to 6
- mesh_rows: bfloat16 [8192, 512], P(('groups', 'band', 'inner')), parts along dimension 0, may hold values from -6 to 6
- edge_source: int32 [8, 4, 3, 4, 128], P(('groups', 'band'), 'inner'), parts along dimension 0, may hold values from 0 to 1023
- edge_target: int32 [8, 4, 3, 4, 128], P(('groups', 'band'), 'inner'), parts along dimension 0, may hold values from 0 to 255
- edge_count: int32 [8, 4, 3, 4], P(('groups', 'band'), 'inner'), parts along dimension 0, may hold values from 0 to 128, as said below
- w_message: bfloat16 [512, 512], replicated, may hold values from -0.25 to 0.25
- w_merge: bfloat16 [512, 512], replicated, may hold values from -0.25 to 0.25
- gain_attn: float32 [512], replicated, may hold values from 0.1 to 1.9
- w_qkv: bfloat16 [512, 1536], replicated, may hold values from -5 to 5
- window: int32 [32], P('groups'), parts along dimension 0, may hold values from 32 to 512, as said below
- w_out: bfloat16 [512, 512], replicated, may hold values from -0.25 to 0.25
- gain_mlp: float32 [512], replicated, may hold values from 0.1 to 1.9
- w_up: bfloat16 [512, 2048], replicated, may hold values from -0.25 to 0.25
- w_down: bfloat16 [2048, 512], replicated, may hold values from -0.125 to 0.125
Outputs:
- mesh_out: bfloat16 [8192, 512], P(('groups', 'band', 'inner')), parts along dimension 0
There are 2 independent parts, one for each index of `groups`. A program takes and returns all parts, laid end to end along the dimension named above; an argument that names none is the same for every part. Nothing has to cross between parts.
Inputs may be any that keep to these rules, and one draw needn't show every extreme that they name: `edge_count`: entries whose target band b + o - 1 lies outside the bands are 0; on every device some block with o = 1 is full (128). Each window is 512 divided by a power of two of at most 16; some head has exactly 512.
All inputs are finite; a program needn't handle non-finite values.
Results may differ from a plain program's by a relative error of at most 0.0061.
Values may be sent and summed in bfloat16 or wider, within the bound.
No kernel may reach another device: no remote copies, remote signals or barrier semaphores. Data moves between devices by JAX's collectives and lax.ppermute only.
A program may use at most 128 MiB of HBM per device.

v0:
```python
import math

import jax
import jax.numpy as jnp
from jax import lax
from jax.sharding import PartitionSpec as P

HEADS = 16
WMAX = 512


norm_eps = 1e-05


def shifted(block, axis, distance):
    devices = range(lax.axis_size(axis))
    route = [(i - distance, i) for i in devices if i - distance in devices]
    return lax.ppermute(block, axis, route)


def extended(cells, sides, width):
    for axis, dim in sides:
        count = lax.axis_size(axis)
        ends = count - 1
        head = lax.slice_in_dim(cells, 0, width, axis=dim)
        tail = lax.slice_in_dim(cells, cells.shape[dim] - width, cells.shape[dim], axis=dim)
        cells = jnp.concatenate(
            [
                lax.ppermute(tail, axis, [(i, (i + 1) % count) for i in range(ends)]),
                cells,
                lax.ppermute(head, axis, [((i + 1) % count, i) for i in range(ends)]),
            ],
            axis=dim,
        )
    return cells


def layer_norm(values, gain):
    center = values - jnp.mean(values, axis=-1, keepdims=True)
    spread = jnp.mean(center * center, axis=-1, keepdims=True)
    return center * lax.rsqrt(spread + norm_eps) * gain


def windowed(queries, padded, windows, base, total_nodes):
    row_count = queries.shape[0]
    head_count = queries.shape[1]
    head_dim = queries.shape[2]
    qblock = math.gcd(512, row_count)
    scale = head_dim ** (-0.5)

    def attend(start):
        block_q = lax.dynamic_slice_in_dim(queries, start, qblock, 0)
        block_kv = lax.dynamic_slice_in_dim(padded, start, qblock + 2 * WMAX, 0)
        scores = (
            jnp.einsum(
                "qhd,khd->hqk", block_q, block_kv[:, :, 0, :], preferred_element_type=jnp.float32
            )
            * scale
        )
        qpos = base + start + jnp.arange(qblock, dtype=jnp.int32)
        kpos = base + start - WMAX + jnp.arange(qblock + 2 * WMAX, dtype=jnp.int32)
        gap = jnp.abs(qpos[:, None] - kpos[None, :])
        inside = (kpos >= 0) & (kpos < total_nodes)
        visible = (gap[None, :, :] <= windows[:, None, None]) & inside[None, None, :]
        scores = jnp.where(visible, scores, -1e30)
        maximum = jnp.max(scores, axis=-1, keepdims=True)
        expo = jnp.where(visible, jnp.exp(scores - maximum), 0.0)
        probs = (expo / jnp.sum(expo, axis=-1, keepdims=True)).astype(jnp.bfloat16)
        return jnp.einsum(
            "hqk,khd->qhd", probs, block_kv[:, :, 1, :], preferred_element_type=jnp.float32
        ).astype(jnp.bfloat16)

    starts = jnp.arange(row_count // qblock, dtype=jnp.int32) * qblock
    return lax.map(attend, starts).reshape(row_count, head_count * head_dim)


def local(
    grid_rows,
    mesh_rows,
    edge_source,
    edge_target,
    edge_count,
    w_message,
    w_merge,
    gain_attn,
    w_qkv,
    window,
    w_out,
    gain_mlp,
    w_up,
    w_down,
):
    band_count = lax.axis_size("band")
    inner_count = lax.axis_size("inner")
    band_index = lax.axis_index("band")
    inner_index = lax.axis_index("inner")
    mesh_dev = mesh_rows.shape[0]
    width = mesh_rows.shape[1]
    slot_cap = edge_source.shape[-1]
    message_rows = jax.nn.silu(
        jnp.dot(grid_rows, w_message, preferred_element_type=jnp.float32)
    ).astype(jnp.bfloat16)
    sources = edge_source.reshape(3, inner_count, slot_cap)
    counts = edge_count.reshape(3, inner_count)
    live = lax.broadcasted_iota(jnp.int32, (3, inner_count, slot_cap), 2) < counts[:, :, None]
    targets = jnp.where(live, edge_target.reshape(3, inner_count, slot_cap), mesh_dev)
    outgoing = jnp.take(message_rows, sources.reshape(-1), axis=0).reshape(
        3, inner_count, slot_cap, width
    )
    came_up, came_up_t = shifted((outgoing[2], targets[2]), "band", 1)
    came_down, came_down_t = shifted((outgoing[0], targets[0]), "band", -1)
    in_band = jnp.stack([came_up, outgoing[1], came_down])
    in_band_t = jnp.stack([came_up_t, targets[1], came_down_t])
    received, received_t = (
        lax.all_to_all(in_band, "inner", split_axis=1, concat_axis=1, tiled=True),
        lax.all_to_all(in_band_t, "inner", split_axis=1, concat_axis=1, tiled=True),
    )
    flat_rows = received.reshape(-1, width)
    flat_targets = received_t.reshape(-1)
    onehot = (
        lax.broadcasted_iota(jnp.int32, (mesh_dev, flat_targets.shape[0]), 0)
        == flat_targets[None, :]
    ).astype(jnp.bfloat16)
    aggregated = jnp.dot(onehot, flat_rows, preferred_element_type=jnp.float32).astype(jnp.bfloat16)
    mesh_state = mesh_rows.astype(jnp.float32) + jnp.dot(
        aggregated, w_merge, preferred_element_type=jnp.float32
    )
    normed = layer_norm(mesh_state, gain_attn).astype(jnp.bfloat16)
    head_dim = width // HEADS
    total_nodes = band_count * inner_count * mesh_dev
    heads_dev = HEADS // inner_count
    own_cols = heads_dev * 3 * head_dim
    w_own = lax.dynamic_slice_in_dim(w_qkv, inner_index * own_cols, own_cols, 1)
    band_qkv = jnp.dot(
        lax.all_gather(normed, "inner", axis=0, tiled=True),
        w_own,
        preferred_element_type=jnp.float32,
    ).astype(jnp.bfloat16)
    band_tokens = band_qkv.shape[0]
    grouped = band_qkv.reshape(band_tokens, heads_dev, 3, head_dim)
    queries = grouped[:, :, 0, :]
    keyval = grouped[:, :, 1:, :].reshape(band_tokens, heads_dev * 2 * head_dim)
    padded = extended(keyval, (("band", 0),), WMAX)
    padded = padded.reshape(band_tokens + 2 * WMAX, heads_dev, 2, head_dim)
    windows = lax.dynamic_slice_in_dim(window, inner_index * heads_dev, heads_dev, 0)
    attended = windowed(queries, padded, windows, band_index * band_tokens, total_nodes)
    w_rows = lax.dynamic_slice_in_dim(
        w_out, inner_index * heads_dev * head_dim, heads_dev * head_dim, 0
    )
    mixed = lax.psum_scatter(
        jnp.dot(attended, w_rows, preferred_element_type=jnp.float32),
        "inner",
        scatter_dimension=0,
        tiled=True,
    )
    mid = mesh_state + mixed
    normed_mlp = layer_norm(mid, gain_mlp).astype(jnp.bfloat16)
    hidden = jax.nn.silu(jnp.dot(normed_mlp, w_up, preferred_element_type=jnp.float32)).astype(
        jnp.bfloat16
    )
    return (mid + jnp.dot(hidden, w_down, preferred_element_type=jnp.float32)).astype(jnp.bfloat16)


def solution(mesh):
    placed = (
        P(("groups", "band", "inner"), None),
        P(("groups", "band", "inner"), None),
        P(("groups", "band"), "inner", None, None, None),
        P(("groups", "band"), "inner", None, None, None),
        P(("groups", "band"), "inner", None, None),
        P(),
        P(),
        P(),
        P(),
        P("groups"),
        P(),
        P(),
        P(),
        P(),
    )
    return jax.shard_map(
        local,
        mesh=mesh,
        in_specs=placed,
        out_specs=P(("groups", "band", "inner"), None),
        check_vma=False,
    )
```

profile of v0, /device:TPU:15, one launch (start us, length us, event | category | flops | bytes accessed | tf_op | source)
XLA Modules:
  0.0 213.0 jit_solution(14507250431289225649)
XLA Ops:
  10.5 5.4 %gather_fusion = bf16[1536,512]{1,0:T(8,128)(2,1)} fusion(bf16[1024,512]{1,0:T(8,128)(2,1)S(1)} %multiply_convert_fusion.1, s32[2048]{0:T(1024)S(1)} %pad_clamp_fusion), kind=kCustom, calls=%fused_computation | custom fusion | bytes 3151872 | tf_op jit(solution)/shard_map/jit(_take)/gather | solution.py:107
  18.5 3.2 %collective-permute-start.2 = (bf16[4,128,512]{2,1,0:T(8,128)(2,1)}, bf16[4,128,512]{2,1,0:T(8,128)(2,1)}, u32[]{:S(2)}, u32[]{:S(2)}) collective-permute-start(bf16[4,128,512]{2,1,0:T(8,128)(2,1)} %bitcast.13), channel_id=1, source_target_pairs={{0,4},{4,8},{8,12},{1,5},{5,9},{9,13},{2,6},{6,10},{10,14},{3,7},{... | collective-permute-start | bytes 1572872 | tf_op jit(solution)/shard_map/ppermute | solution.py:18
  21.7 2.9 %collective-permute-start.3 = (bf16[4,128,512]{2,1,0:T(8,128)(2,1)S(1)}, bf16[4,128,512]{2,1,0:T(8,128)(2,1)}, u32[]{:S(2)}, u32[]{:S(2)}) collective-permute-start(bf16[4,128,512]{2,1,0:T(8,128)(2,1)S(1)} %bitcast.83), channel_id=1, source_target_pairs={{4,0},{8,4},{12,8},{5,1},{9,5},{13,9},{6,2},{10,6},{14,10},{7,3},{... | collective-permute-start | bytes 1572872 | tf_op jit(solution)/shard_map/ppermute | solution.py:18
  26.6 3.4 %collective-permute-start = (s32[4,128]{1,0:T(4,128)S(1)}, s32[4,128]{1,0:T(4,128)S(1)}, u32[]{:S(2)}, u32[]{:S(2)}) collective-permute-start(s32[4,128]{1,0:T(4,128)S(1)} %get-tuple-element.120), channel_id=1, source_target_pairs={{0,4},{4,8},{8,12},{1,5},{5,9},{9,13},{2,6},{6,10},{10,14},{3,7},{... | collective-permute-start | bytes 6152 | tf_op jit(solution)/shard_map/ppermute | solution.py:18
  30.0 6.3 %collective-permute-done.1 = s32[4,128]{1,0:T(4,128)S(1)} collective-permute-done((s32[4,128]{1,0:T(4,128)S(1)}, s32[4,128]{1,0:T(4,128)S(1)}, u32[]{:S(2)}, u32[]{:S(2)}) %collective-permute-start.1) | collective-permute-done | bytes 2080 | tf_op jit(solution)/shard_map/ppermute | solution.py:18
  36.8 5.2 %all-to-all-start = ((s32[3,4,128]{2,0,1:T(4,128)}), s32[3,4,128]{2,0,1:T(4,128)S(1)}, u32[]{:S(2)}, u32[]{:S(2)}) async-start(s32[3,4,128]{2,0,1:T(4,128)} %pad_add_fusion), calls=%async_computation | async-start | bytes 16384 | tf_op jit(solution)/shard_map/all_to_all | solution.py:116
  42.1 2.5 %pad_maximum_fusion = bf16[3,4,128,512]{3,2,0,1:T(8,128)(2,1)} fusion(bf16[1,4,128,512]{3,2,0,1:T(8,128)(2,1)} %bitcast.18, bf16[1,4,128,512]{3,2,0,1:T(8,128)(2,1)S(1)} %bitcast.79, bf16[1,4,128,512]{3,2,0,1:T(8,128)(2,1)} %bitcast.14), kind=kLoop, calls=%fused_computation.33 | loop fusion | flops 1572864 | bytes 3145728 | tf_op jit(solution)/shard_map/stack | solution.py:112
  44.6 5.6 %all-to-all-start.1 = ((bf16[3,4,128,512]{3,2,0,1:T(8,128)(2,1)}), bf16[3,4,128,512]{3,2,0,1:T(8,128)(2,1)}, u32[]{:S(2)}, u32[]{:S(2)}) async-start(bf16[3,4,128,512]{3,2,0,1:T(8,128)(2,1)} %pad_maximum_fusion), calls=%async_computation.1 | async-start | bytes 3145728 | tf_op jit(solution)/shard_map/all_to_all | solution.py:115
  50.2 18.3 %all-to-all-done.1 = bf16[3,4,128,512]{3,2,0,1:T(8,128)(2,1)} async-done(((bf16[3,4,128,512]{3,2,0,1:T(8,128)(2,1)}), bf16[3,4,128,512]{3,2,0,1:T(8,128)(2,1)}, u32[]{:S(2)}, u32[]{:S(2)}) %all-to-all-start.1) | async-done | bytes 1572896 | tf_op jit(solution)/shard_map/all_to_all | solution.py:115
  68.5 2.7 %copy.34 = bf16[3,4,128,512]{3,2,1,0:T(8,128)(2,1)} copy(bf16[3,4,128,512]{3,2,0,1:T(8,128)(2,1)} %all-to-all-done.1) | data formatting | bytes 3145728 | tf_op jit(solution)/shard_map/all_to_all | solution.py:115
  71.1 2.4 %fusion.48 = (f32[256]{0:T(256)S(1)}, f32[256,512]{1,0:T(8,128)S(1)}) fusion(bf16[512,512]{1,0:T(8,128)(2,1)} %param.22, bf16[1536,512]{1,0:T(8,128)(2,1)} %bitcast.80, s32[1536]{0:T(1024)S(1)} %eq.10, bf16[256,512]{1,0:T(8,128)(2,1)S(1)} %copy-done.8), kind=kOutput, calls=%fused_computation.80 | convolution fusion | flops 537788160 | bytes 2890752 | tf_op jit(solution)/shard_map/dot_general | solution.py:125
  74.7 16.5 %all-gather.2.cloned.1.call-done = bf16[1024,512]{1,0:T(8,128)(2,1)} async-done(((bf16[256,512]{1,0:T(8,128)(2,1)}), bf16[1024,512]{1,0:T(8,128)(2,1)}) %all-gather.2.cloned.1.call-update) | async-done | bytes 1048592 | tf_op jit(solution)/shard_map/all_gather | solution.py:135
  94.0 3.1 %collective-permute-start.4 = (bf16[512,256]{0,1:T(8,128)(2,1)}, bf16[512,256]{0,1:T(8,128)(2,1)S(1)}, u32[]{:S(2)}, u32[]{:S(2)}) collective-permute-start(bf16[512,256]{0,1:T(8,128)(2,1)} %bitcast.21), channel_id=1, source_target_pairs={{0,4},{4,8},{8,12},{1,5},{5,9},{9,13},{2,6},{6,10},{10,14},{3,7},{... | collective-permute-start | bytes 786440 | tf_op jit(solution)/shard_map/ppermute | solution.py:29
  97.1 2.4 %collective-permute-start.5 = (bf16[512,256]{0,1:T(8,128)(2,1)}, bf16[512,256]{0,1:T(8,128)(2,1)S(1)}, u32[]{:S(2)}, u32[]{:S(2)}) collective-permute-start(bf16[512,256]{0,1:T(8,128)(2,1)} %bitcast.23), channel_id=1, source_target_pairs={{4,0},{8,4},{12,8},{5,1},{9,5},{13,9},{6,2},{10,6},{14,10},{7,3},{... | collective-permute-start | bytes 786440 | tf_op jit(solution)/shard_map/ppermute | solution.py:31
  100.4 3.4 %collective-permute-done.4 = bf16[512,256]{0,1:T(8,128)(2,1)S(1)} collective-permute-done((bf16[512,256]{0,1:T(8,128)(2,1)}, bf16[512,256]{0,1:T(8,128)(2,1)S(1)}, u32[]{:S(2)}, u32[]{:S(2)}) %collective-permute-start.4) | collective-permute-done | bytes 262176 | tf_op jit(solution)/shard_map/ppermute | solution.py:29
  103.8 2.8 %collective-permute-done.5 = bf16[512,256]{0,1:T(8,128)(2,1)S(1)} collective-permute-done((bf16[512,256]{0,1:T(8,128)(2,1)}, bf16[512,256]{0,1:T(8,128)(2,1)S(1)}, u32[]{:S(2)}, u32[]{:S(2)}) %collective-permute-start.5) | collective-permute-done | bytes 262176 | tf_op jit(solution)/shard_map/ppermute | solution.py:31
  108.4 57.2 %while.12 = (s32[]{:T(128)}, bf16[2,512,4,32]{1,3,2,0:T(8,128)(2,1)}, s32[2]{0:T(128)S(1)}, bf16[2048,4,2,32]{0,3,2,1:T(8,128)(2,1)S(1)}, s32[]{:T(128)}, /*inde...) while((s32[]{:T(128)}, ...), condition=%wide.region_5.6_spmd, body=%wide.region_2.5_spmd.sunk | while | flops 438904320 | bytes 38837480 | solution.py:74
  115.7 14.1 %fusion.63 = (f32[4,512]{1,0:T(4,128)}, f32[4,512,1536]{2,1,0:T(8,128)}) fusion(s32[512,1536]{1,0:T(8,128)} %subtract_abs_fusion.2, s32[4]{0:T(128)S(1)} %get-tuple-element.205, pred[1536]{0:T(1024)(128)(4,1)S(1)} %compare_and_fusion.4, bf16[1536,4,1,32]{0,3,2,1:T(8,128)(2,1)} %get-tuple-element.172, bf16[1024,4,32]{0,2,1:T(8,128)(2,1)} %get-tuple-element.206, ...), kind=kOutput, calls=%fused_computation.77.clone.1 | convolution fusion | flops 229639680 | bytes 19411972 | tf_op jit(solution)/shard_map/while/body/eval_jaxpr/sub | solution.py:67
  129.7 7.3 %fusion.64 = bf16[2,512,4,32]{1,3,2,0:T(8,128)(2,1)} fusion(bf16[2,512,4,32]{1,3,2,0:T(8,128)(2,1)} %get-tuple-element.189, s32[]{:T(128)} %get-tuple-element.188, f32[4,512,1536]{2,1,0:T(8,128)} %get-tuple-element.173, f32[4,512]{1,0:T(4,128)} %get-tuple-element.174, bf16[1536,4,1,32]{0,3,2,1:T(8,128)(2,1)S(1)} %get-tuple-element.175), kind=kOutput, calls=%fused_computation.17.clone.1 | convolution fusion | flops 207683584 | bytes 13115904 | tf_op jit(solution)/shard_map/while/body/eval_jaxpr/hqk,khd->qhd/dot_general | solution.py:69
  144.3 14.0 %fusion.63 = (f32[4,512]{1,0:T(4,128)}, f32[4,512,1536]{2,1,0:T(8,128)}) fusion(s32[512,1536]{1,0:T(8,128)} %subtract_abs_fusion.2, s32[4]{0:T(128)S(1)} %get-tuple-element.205, pred[1536]{0:T(1024)(128)(4,1)S(1)} %compare_and_fusion.4, bf16[1536,4,1,32]{0,3,2,1:T(8,128)(2,1)} %get-tuple-element.172, bf16[1024,4,32]{0,2,1:T(8,128)(2,1)} %get-tuple-element.206, ...), kind=kOutput, calls=%fused_computation.77.clone.1 | convolution fusion | flops 229639680 | bytes 19411972 | tf_op jit(solution)/shard_map/while/body/eval_jaxpr/sub | solution.py:67
  158.3 7.3 %fusion.64 = bf16[2,512,4,32]{1,3,2,0:T(8,128)(2,1)} fusion(bf16[2,512,4,32]{1,3,2,0:T(8,128)(2,1)} %get-tuple-element.189, s32[]{:T(128)} %get-tuple-element.188, f32[4,512,1536]{2,1,0:T(8,128)} %get-tuple-element.173, f32[4,512]{1,0:T(4,128)} %get-tuple-element.174, bf16[1536,4,1,32]{0,3,2,1:T(8,128)(2,1)S(1)} %get-tuple-element.175), kind=kOutput, calls=%fused_computation.17.clone.1 | convolution fusion | flops 207683584 | bytes 13115904 | tf_op jit(solution)/shard_map/while/body/eval_jaxpr/hqk,khd->qhd/dot_general | solution.py:69
  166.9 2.8 %fusion.35 = f32[1024,512]{1,0:T(8,128)} fusion(bf16[1024,128]{0,1:T(8,128)(2,1)S(1)} %bitcast.82, bf16[512,512]{1,0:T(8,128)(2,1)} %param.26, s32[]{:T(128)S(6)} %select_n.64), kind=kOutput, calls=%fused_computation.54 | convolution fusion | flops 134217728 | bytes 2490372 | tf_op jit(solution)/shard_map/dot_general | solution.py:151
  169.7 31.4 %reduce-scatter.2.cloned.1.call-done = f32[256,512]{1,0:T(8,128)} async-done(((f32[1024,512]{1,0:T(8,128)}), f32[256,512]{1,0:T(8,128)}) %reduce-scatter.2.cloned.1.call-update) | async-done | bytes 524304 | tf_op jit(solution)/shard_map/reduce_scatter | solution.py:150
  202.5 3.7 %fusion.23 = bf16[256,512]{1,0:T(8,128)(2,1)} fusion(f32[256,512]{1,0:T(8,128)S(1)} %get-tuple-element.110, bf16[2048,512]{1,0:T(8,128)(2,1)S(1)} %copy-done, bf16[512,2048]{1,0:T(8,128)(2,1)} %param.28, f32[512]{0:T(512)S(1)} %copy-done.9, f32[256]{0:T(256)S(1)} %add_rsqrt_fusion, f32[256]{0:T(256)S(1)} %broadcast_multiply_fusion), kind=kOutput, calls=%fused_computation.40 | convolution fusion | flops 1077149696 | bytes 4984832 | tf_op jit(solution)/shard_map/dot_general | solution.py:161
  (76 shorter events, 26.1 us)
Async XLA Ops:
  6.5 195.9 %copy-start = (bf16[2048,512]{1,0:T(8,128)(2,1)S(1)}, bf16[2048,512]{1,0:T(8,128)(2,1)}, u32[]{:S(2)}) copy-start(bf16[2048,512]{1,0:T(8,128)(2,1)} %param.29) | copy-start | bytes 6291460
  17.6 7.0 %copy-start.7 = (s32[1,1,3,4]{3,1,2,0:T(1,128)S(1)}, s32[1,1,3,4]{3,1,2,0:T(1,128)}, u32[]{:S(2)}) copy-start(s32[1,1,3,4]{3,1,2,0:T(1,128)} %param.20) | copy-start | bytes 148
  17.6 7.0 %copy-start.5 = (s32[1,1,3,4,128]{4,3,2,1,0:T(4,128)S(1)}, s32[1,1,3,4,128]{4,3,2,1,0:T(4,128)}, u32[]{:S(2)}) copy-start(s32[1,1,3,4,128]{4,3,2,1,0:T(4,128)} %param.19) | copy-start | bytes 18436
  18.5 23.6 %collective-permute-start.2 = (bf16[4,128,512]{2,1,0:T(8,128)(2,1)}, bf16[4,128,512]{2,1,0:T(8,128)(2,1)}, u32[]{:S(2)}, u32[]{:S(2)}) collective-permute-start(bf16[4,128,512]{2,1,0:T(8,128)(2,1)} %bitcast.13), channel_id=1, source_target_pairs={{0,4},{4,8},{8,12},{1,5},{5,9},{9,13},{2,6},{6,10},{10,14},{3,7},{... | collective-permute-start | bytes 1572872 | tf_op jit(solution)/shard_map/ppermute | solution.py:18
  21.7 20.4 %collective-permute-start.3 = (bf16[4,128,512]{2,1,0:T(8,128)(2,1)S(1)}, bf16[4,128,512]{2,1,0:T(8,128)(2,1)}, u32[]{:S(2)}, u32[]{:S(2)}) collective-permute-start(bf16[4,128,512]{2,1,0:T(8,128)(2,1)S(1)} %bitcast.83), channel_id=1, source_target_pairs={{4,0},{8,4},{12,8},{5,1},{9,5},{13,9},{6,2},{10,6},{14,10},{7,3},{... | collective-permute-start | bytes 1572872 | tf_op jit(solution)/shard_map/ppermute | solution.py:18
  24.7 11.5 %collective-permute-start.1 = (s32[4,128]{1,0:T(4,128)S(1)}, s32[4,128]{1,0:T(4,128)S(1)}, u32[]{:S(2)}, u32[]{:S(2)}) collective-permute-start(s32[4,128]{1,0:T(4,128)S(1)} %get-tuple-element.121), channel_id=1, source_target_pairs={{4,0},{8,4},{12,8},{5,1},{9,5},{13,9},{6,2},{10,6},{14,10},{7,3},{... | collective-permute-start | bytes 6152 | tf_op jit(solution)/shard_map/ppermute | solution.py:18
  26.6 9.6 %collective-permute-start = (s32[4,128]{1,0:T(4,128)S(1)}, s32[4,128]{1,0:T(4,128)S(1)}, u32[]{:S(2)}, u32[]{:S(2)}) collective-permute-start(s32[4,128]{1,0:T(4,128)S(1)} %get-tuple-element.120), channel_id=1, source_target_pairs={{0,4},{4,8},{8,12},{1,5},{5,9},{9,13},{2,6},{6,10},{10,14},{3,7},{... | collective-permute-start | bytes 6152 | tf_op jit(solution)/shard_map/ppermute | solution.py:18
  36.8 7.8 %all-to-all-start = ((s32[3,4,128]{2,0,1:T(4,128)}), s32[3,4,128]{2,0,1:T(4,128)S(1)}, u32[]{:S(2)}, u32[]{:S(2)}) async-start(s32[3,4,128]{2,0,1:T(4,128)} %pad_add_fusion), calls=%async_computation | async-start | bytes 16384 | tf_op jit(solution)/shard_map/all_to_all | solution.py:116
  44.6 23.9 %all-to-all-start.1 = ((bf16[3,4,128,512]{3,2,0,1:T(8,128)(2,1)}), bf16[3,4,128,512]{3,2,0,1:T(8,128)(2,1)}, u32[]{:S(2)}, u32[]{:S(2)}) async-start(bf16[3,4,128,512]{3,2,0,1:T(8,128)(2,1)} %pad_maximum_fusion), calls=%async_computation.1 | async-start | bytes 3145728 | tf_op jit(solution)/shard_map/all_to_all | solution.py:115
  50.2 20.9 %copy-start.8 = (bf16[256,512]{1,0:T(8,128)(2,1)S(1)}, bf16[256,512]{1,0:T(8,128)(2,1)}, u32[]{:S(2)}) copy-start(bf16[256,512]{1,0:T(8,128)(2,1)} %param.17) | copy-start | bytes 786436
  50.2 41.1 %all-gather.2.cloned.1.call-start = ((), (), s32[]{:S(2)}) async-start(), calls=%async_computation.3 | async-start | bytes 1310720 | tf_op jit(solution)/shard_map/all_gather | solution.py:135
  71.1 2.6 %copy-start.6 = (f32[512]{0:T(512)S(1)}, f32[512]{0:T(512)}, u32[]{:S(2)}) copy-start(f32[512]{0:T(512)} %param.23) | copy-start | bytes 6148
  73.5 20.5 %copy-start.1 = (f32[256,512]{1,0:T(8,128)}, f32[256,512]{1,0:T(8,128)S(1)}, u32[]{:S(2)}) copy-start(f32[256,512]{1,0:T(8,128)S(1)} %get-tuple-element.124) | copy-start | bytes 1572868
  73.8 25.8 %copy-start.10 = (s32[16]{0:T(128)S(1)}, s32[16]{0:T(128)}, u32[]{:S(2)}) copy-start(s32[16]{0:T(128)} %param.25) | copy-start | bytes 196
  74.7 126.4 %reduce-scatter.2.cloned.1.call-start = ((), (), s32[]{:S(2)}) async-start(), calls=%async_computation.4 | async-start | bytes 2621440 | tf_op jit(solution)/shard_map/reduce_scatter | solution.py:150
  94.0 9.7 %collective-permute-start.4 = (bf16[512,256]{0,1:T(8,128)(2,1)}, bf16[512,256]{0,1:T(8,128)(2,1)S(1)}, u32[]{:S(2)}, u32[]{:S(2)}) collective-permute-start(bf16[512,256]{0,1:T(8,128)(2,1)} %bitcast.21), channel_id=1, source_target_pairs={{0,4},{4,8},{8,12},{1,5},{5,9},{9,13},{2,6},{6,10},{10,14},{3,7},{... | collective-permute-start | bytes 786440 | tf_op jit(solution)/shard_map/ppermute | solution.py:29
  97.1 9.4 %collective-permute-start.5 = (bf16[512,256]{0,1:T(8,128)(2,1)}, bf16[512,256]{0,1:T(8,128)(2,1)S(1)}, u32[]{:S(2)}, u32[]{:S(2)}) collective-permute-start(bf16[512,256]{0,1:T(8,128)(2,1)} %bitcast.23), channel_id=1, source_target_pairs={{4,0},{8,4},{12,8},{5,1},{9,5},{13,9},{6,2},{10,6},{14,10},{7,3},{... | collective-permute-start | bytes 786440 | tf_op jit(solution)/shard_map/ppermute | solution.py:31
  103.8 2.8 %copy-start.3 = (bf16[512,256]{0,1:T(8,128)(2,1)}, bf16[512,256]{0,1:T(8,128)(2,1)S(1)}, u32[]{:S(2)}) copy-start(bf16[512,256]{0,1:T(8,128)(2,1)S(1)} %collective-permute-done.4) | copy-start | bytes 786436
  106.6 0.7 copy-start.4
  166.9 34.2 %copy-start.2 = (f32[256,512]{1,0:T(8,128)S(1)}, f32[256,512]{1,0:T(8,128)}, u32[]{:S(2)}) copy-start(f32[256,512]{1,0:T(8,128)} %copy-done.1) | copy-start | bytes 1572868
  169.7 32.8 %copy-start.9 = (f32[512]{0:T(512)S(1)}, f32[512]{0:T(512)}, u32[]{:S(2)}) copy-start(f32[512]{0:T(512)} %param.27) | copy-start | bytes 6148
Sparse Core Ops, SparseCore 0:
  74.8 16.4 all-gather.1
  169.8 31.2 reduce-scatter.1
where the time goes:
time: 216 us; the launch traced here: 213 us
  waiting for transfers between devices  78.6 us (36%)
  matrix products  55.8 us (26%)
  starting transfers between devices  27.6 us (13%)
  local copies, waits for them, and re-layouts  17 us (8%)
  between operations  13.7 us (6%)
  other arithmetic  13.4 us (6%)
  loops' own time  6.82 us (3%)
    reduce_scatter x1, waiting for transfers between devices, local(): lax.psum_scatter(jnp.dot(attended, w_rows, preferred_element_type=jnp.flo...  31.4 us
    sub x2, matrix products, attend(): expo = jnp.where(visible, jnp.exp(scores - maximum), 0.0)  28.1 us
    all_to_all x1, waiting for transfers between devices, local(): lax.all_to_all(in_band, 'inner', split_axis=1, concat_axis=1, tiled=True)  18.3 us
    all_gather x1, waiting for transfers between devices, local(): lax.all_gather(normed, 'inner', axis=0, tiled=True)  16.5 us
    dot_general x2, matrix products, attend(): jnp.einsum('hqk,khd->qhd', probs, block_kv[:, :, 1, :], preferred_element...  14.6 us
    ppermute x4, starting transfers between devices, shifted(): return lax.ppermute(block, axis, route)  11.3 us
    another operation x1, loops' own time, windowed(): return lax.map(attend, starts).reshape(row_count, head_count * head_dim)  6.82 us
    ppermute x4, waiting for transfers between devices, shifted(): return lax.ppermute(block, axis, route)  6.26 us
  transfers between devices with their start and end apart: 10, of which 6 were waited for; matrix products, arithmetic and copies ran while one was open for 2% of the time, Pallas kernels for 0%

commit v1 on v0

v1 whole, which is shorter than its diff:
```python
import functools
import math

import jax
import jax.numpy as jnp
from jax import lax
from jax.experimental import pallas as pl
from jax.experimental.pallas import tpu as pltpu
from jax.sharding import PartitionSpec as P

HEADS = 16
WMAX = 512
LANES = 128
NEAR = 128

norm_eps = 1e-05
NODES = ("band", "inner")
VMEM = pl.BlockSpec(memory_space=pltpu.VMEM)
SMEM = pl.BlockSpec(memory_space=pltpu.SMEM)


def params(mib):
    return pltpu.CompilerParams(vmem_limit_bytes=mib * 1024 * 1024)


def dot(a, b):
    return jnp.dot(a, b, preferred_element_type=jnp.float32)


def dot_t(a, b):
    return lax.dot_general(a, b, (((1,), (1,)), ((), ())), preferred_element_type=jnp.float32)


def layer_norm(values, gain):
    center = values - jnp.mean(values, axis=-1, keepdims=True)
    spread = jnp.mean(center * center, axis=-1, keepdims=True)
    return center * lax.rsqrt(spread + norm_eps) * gain


def message_kernel(inner_count, grid_ref, w_ref, source_ref, *out_refs):
    rows = grid_ref.shape[0]
    blocks, cap = source_ref.shape
    message = jax.nn.silu(dot(grid_ref[...], w_ref[...])).astype(jnp.bfloat16)
    inner = lax.axis_index("inner")
    sources = jnp.concatenate(
        [
            source_ref[pl.ds(o * inner_count + (inner ^ d), 1), :]
            for o in range(3)
            for d in range(inner_count)
        ],
        axis=0,
    )
    by_slot = jnp.transpose(sources.astype(jnp.float32)).astype(jnp.int32)
    row = lax.broadcasted_iota(jnp.int32, (cap, rows), 1)
    step = math.gcd(blocks, 4)
    for first in range(0, blocks, step):
        picks = jnp.concatenate(
            [
                jnp.where(row == by_slot[:, n : n + 1], 1.0, 0.0).astype(jnp.bfloat16)
                for n in range(first, first + step)
            ],
            axis=0,
        )
        taken = dot(picks, message).astype(jnp.bfloat16)
        for n in range(first, first + step):
            out_refs[n][...] = taken[(n - first) * cap : (n - first + 1) * cap]


def merge_kernel(inner_count, band_count, *refs):
    blocks = 3 * inner_count
    row_refs = refs[:blocks]
    target_ref, mesh_ref, w_ref, gain_ref, state_ref, normed_ref = refs[blocks:]
    nodes = mesh_ref.shape[0]
    cap = row_refs[0].shape[0]
    band = lax.axis_index("band")
    inner = lax.axis_index("inner")
    node = lax.broadcasted_iota(jnp.int32, (nodes, cap), 0)
    hits = []
    for o in range(3):
        sender_band = band + 1 - o
        present = (sender_band >= 0) & (sender_band < band_count)
        for d in range(inner_count):
            sender = sender_band * inner_count + (inner ^ d)
            place = jnp.where(present, (sender * 3 + o) * inner_count + inner, 0)
            target = jnp.where(present, target_ref[pl.ds(place, 1), :], -1)
            hits.append(jnp.where(node == target, 1.0, 0.0).astype(jnp.bfloat16))
    aggregated = dot(
        jnp.concatenate(hits, axis=1), jnp.concatenate([r[...] for r in row_refs], axis=0)
    ).astype(jnp.bfloat16)
    state = mesh_ref[...].astype(jnp.float32) + dot(aggregated, w_ref[...])
    state_ref[...] = state
    normed_ref[...] = layer_norm(state, gain_ref[...]).astype(jnp.bfloat16)


def project_keys(rows, wk_ref, wv_ref, key_ref, value_ref, start):
    count = rows.shape[0]
    groups = key_ref.shape[0]
    heads = value_ref.shape[0]
    keys = dot(rows, wk_ref[...]).astype(jnp.bfloat16)
    for g in range(groups):
        key_ref[g, start : start + count, :] = keys[:, g * LANES : (g + 1) * LANES]
    values = dot_t(wv_ref[...], rows).astype(jnp.bfloat16)
    value_ref[:, 0 : values.shape[0] // heads, start : start + count] = values.reshape(
        heads, -1, count
    )


def near_kernel(
    own_ref, side_ref, wq_ref, wk_ref, wv_ref, order_ref, window_ref,
    query_ref, sums_ref, top_ref,
    key_ref, value_ref, gap_ref,
):
    nodes, width = own_ref.shape
    head_dim = width // HEADS
    per_group = LANES // head_dim
    odd = lax.rem(lax.axis_index("inner"), 2)
    side = 1 - 2 * odd
    first = odd * (nodes - NEAR)
    second = (1 - odd) * NEAR
    scale = head_dim ** (-0.5) / math.log(2.0)

    queries = dot_t(wq_ref[...], own_ref[...]).astype(jnp.bfloat16)
    part = lax.broadcasted_iota(jnp.int32, (LANES, nodes), 0) // head_dim
    for h in range(HEADS):
        g = h // per_group
        lanes = queries[g * LANES : (g + 1) * LANES]
        query_ref[h] = jnp.where(part == h % per_group, lanes, jnp.zeros_like(lanes))
    value_ref[:, head_dim:, :] = jnp.ones_like(value_ref[:, head_dim:, :])
    project_keys(own_ref[...], wk_ref, wv_ref, key_ref, value_ref, 0)
    project_keys(side_ref[pl.ds(pl.multiple_of(first, NEAR), NEAR), :], wk_ref, wv_ref, key_ref, value_ref, nodes)
    project_keys(
        side_ref[pl.ds(pl.multiple_of(second, NEAR), NEAR), :], wk_ref, wv_ref, key_ref, value_ref, nodes + NEAR
    )
    lag = lax.broadcasted_iota(jnp.int32, (nodes, nodes), 0) - lax.broadcasted_iota(
        jnp.int32, (nodes, nodes), 1
    )
    gap_ref[0:nodes] = jnp.abs(lag)
    gap_ref[nodes : nodes + NEAR] = jnp.abs(lag[0:NEAR] + (side * nodes + first))
    gap_ref[nodes + NEAR : 2 * nodes] = jnp.abs(lag[0:NEAR] + (side * nodes + second))

    def attend(h, rows):
        scores = dot(key_ref[h // per_group, 0:rows, :], query_ref[h])
        scores = jnp.where(gap_ref[0:rows] <= window_ref[h], scores, -1e30)
        top = jnp.max(scores, axis=0, keepdims=True)
        expo = jnp.exp2((scores - top) * scale).astype(jnp.bfloat16)
        sums_ref[h] = dot(value_ref[h, :, 0:rows], expo)
        top_ref[h] = jnp.broadcast_to(top, top_ref.shape[1:])

    def pair(i, carry):
        a, b = order_ref[2 * i], order_ref[2 * i + 1]
        widest = jnp.maximum(window_ref[a], window_ref[b])

        @pl.when(widest <= NEAR)
        def _():
            attend(a, nodes + NEAR)
            attend(b, nodes + NEAR)

        @pl.when(widest > NEAR)
        def _():
            attend(a, 2 * nodes)
            attend(b, 2 * nodes)

        return carry

    lax.fori_loop(0, HEADS // 2, pair, 0)


def far_kernel(
    beyond_ref, before_ref, after_ref, wk_ref, wv_ref, order_ref, window_ref,
    query_ref, sums_ref, top_ref, state_ref, w_out_ref, gain_ref, up_ref, down_ref,
    out_ref,
    key_ref, value_ref, gap_ref, attended_ref, up_vmem, down_vmem, sems,
):
    nodes, width = beyond_ref.shape
    head_dim = width // HEADS
    per_group = LANES // head_dim
    total = lax.axis_size("band") * lax.axis_size("inner")
    me = lax.axis_index("band") * lax.axis_size("inner") + lax.axis_index("inner")
    odd = lax.rem(lax.axis_index("inner"), 2)
    side = 2 * odd - 1
    first = (1 - odd) * (nodes - NEAR)
    second = odd * NEAR
    scale = head_dim ** (-0.5) / math.log(2.0)
    absent = 1 << 20

    fetch_up = pltpu.make_async_copy(up_ref, up_vmem, sems.at[0])
    fetch_down = pltpu.make_async_copy(down_ref, down_vmem, sems.at[1])
    fetch_up.start()
    fetch_down.start()

    value_ref[:, head_dim:, :] = jnp.ones_like(value_ref[:, head_dim:, :])
    project_keys(beyond_ref[pl.ds(pl.multiple_of(first, NEAR), NEAR), :], wk_ref, wv_ref, key_ref, value_ref, 0)
    project_keys(
        beyond_ref[pl.ds(pl.multiple_of(second, NEAR), NEAR), :], wk_ref, wv_ref, key_ref, value_ref, NEAR
    )
    project_keys(before_ref[...], wk_ref, wv_ref, key_ref, value_ref, nodes)
    project_keys(after_ref[...], wk_ref, wv_ref, key_ref, value_ref, 2 * nodes)
    lag = lax.broadcasted_iota(jnp.int32, (nodes, nodes), 0) - lax.broadcasted_iota(
        jnp.int32, (nodes, nodes), 1
    )

    def gap(rows, device, offset):
        inside = (me + device >= 0) & (me + device < total)
        return jnp.where(inside, jnp.abs(rows + (device * nodes + offset)), absent)

    gap_ref[0:NEAR] = gap(lag[0:NEAR], side, first)
    gap_ref[NEAR:nodes] = gap(lag[0:NEAR], side, second)
    gap_ref[nodes : 2 * nodes] = gap(lag, -2, 0)
    gap_ref[2 * nodes : 3 * nodes] = gap(lag, 2, 0)

    def attend(h, rows):
        scores = dot(key_ref[h // per_group, 0:rows, :], query_ref[h])
        scores = jnp.where(gap_ref[0:rows] <= window_ref[h], scores, -1e30)
        before = top_ref[h, 0:1, :]
        top = jnp.maximum(before, jnp.max(scores, axis=0, keepdims=True))
        expo = jnp.exp2((scores - top) * scale).astype(jnp.bfloat16)
        sums = sums_ref[h] * jnp.exp2((before - top) * scale) + dot(value_ref[h, :, 0:rows], expo)
        attended_ref[h] = (sums[0:head_dim] / sums[head_dim : head_dim + 1]).astype(jnp.bfloat16)

    def pair(i, carry):
        a, b = order_ref[2 * i], order_ref[2 * i + 1]
        widest = jnp.maximum(window_ref[a], window_ref[b])

        @pl.when(widest <= NEAR)
        def _():
            attend(a, NEAR)
            attend(b, NEAR)

        @pl.when((widest > NEAR) & (widest <= nodes))
        def _():
            attend(a, nodes)
            attend(b, nodes)

        @pl.when(widest > nodes)
        def _():
            attend(a, 3 * nodes)
            attend(b, 3 * nodes)

        return carry

    lax.fori_loop(0, HEADS // 2, pair, 0)

    attended = attended_ref[...].reshape(width, nodes)
    mixed = lax.dot_general(
        attended, w_out_ref[...], (((0,), (0,)), ((), ())), preferred_element_type=jnp.float32
    )
    mid = state_ref[...] + mixed
    normed = layer_norm(mid, gain_ref[...]).astype(jnp.bfloat16)
    fetch_up.wait()
    hidden = jax.nn.silu(dot(normed, up_vmem[...])).astype(jnp.bfloat16)
    fetch_down.wait()
    out_ref[...] = (mid + dot(hidden, down_vmem[...])).astype(jnp.bfloat16)


def cost(flops, size):
    return pl.CostEstimate(flops=flops, bytes_accessed=size, transcendentals=0)


def local(
    grid_rows,
    mesh_rows,
    edge_source,
    edge_target,
    edge_count,
    w_message,
    w_merge,
    gain_attn,
    w_qkv,
    window,
    w_out,
    gain_mlp,
    w_up,
    w_down,
):
    bands = lax.axis_size("band")
    inners = lax.axis_size("inner")
    devices = bands * inners
    grid_dev = grid_rows.shape[0]
    nodes, width = mesh_rows.shape
    cap = edge_source.shape[-1]
    head_dim = width // HEADS
    blocks = 3 * inners
    f32, bf16, i32 = jnp.float32, jnp.bfloat16, jnp.int32

    live = lax.broadcasted_iota(i32, (blocks, cap), 1) < edge_count.reshape(blocks)[:, None]
    targets = jnp.where(live, edge_target.reshape(blocks, cap), -1)
    targets = lax.all_gather(targets, NODES, axis=0, tiled=True)

    outgoing = pl.pallas_call(
        functools.partial(message_kernel, inners),
        out_shape=[jax.ShapeDtypeStruct((cap, width), bf16)] * blocks,
        in_specs=[VMEM] * 3,
        out_specs=[VMEM] * blocks,
        compiler_params=params(24),
        cost_estimate=cost(2 * grid_dev * width * (width + blocks * cap), 4 << 20),
        name="messages",
    )(grid_rows, w_message, edge_source.reshape(blocks, cap))

    arrived = []
    for o in range(3):
        for d in range(inners):
            route = [
                (b * inners + i, (b + o - 1) * inners + (i ^ d))
                for b in range(bands)
                for i in range(inners)
                if 0 <= b + o - 1 < bands
            ]
            block = outgoing[o * inners + d]
            arrived.append(block if o == 1 and d == 0 else lax.ppermute(block, NODES, route))

    w_parts = w_qkv.reshape(width, HEADS, 3, head_dim)
    w_query = w_parts[:, :, 0].reshape(width, width).T
    w_key = w_parts[:, :, 1].reshape(width, width)
    w_value = w_parts[:, :, 2].reshape(width, width).T
    ahead = (window[None, :] > window[:, None]) | (
        (window[None, :] == window[:, None]) & (jnp.arange(HEADS)[None, :] < jnp.arange(HEADS)[:, None])
    )
    rank = jnp.sum(ahead.astype(i32), axis=1)
    order = jnp.sum(
        jnp.where(rank[None, :] == jnp.arange(HEADS)[:, None], jnp.arange(HEADS)[None, :], 0), axis=1
    ).astype(i32)

    state, normed = pl.pallas_call(
        functools.partial(merge_kernel, inners, bands),
        out_shape=[
            jax.ShapeDtypeStruct((nodes, width), f32),
            jax.ShapeDtypeStruct((nodes, width), bf16),
        ],
        in_specs=[VMEM] * (blocks + 4),
        out_specs=[VMEM] * 2,
        compiler_params=params(24),
        cost_estimate=cost(2 * nodes * width * (width + blocks * cap), 4 << 20),
        name="merge",
    )(*arrived, targets, mesh_rows, w_merge, gain_attn.reshape(1, width))

    side = lax.ppermute(normed, NODES, [(g, g ^ 1) for g in range(devices)])
    beyond = lax.ppermute(
        normed,
        NODES,
        [(g, g + 1) for g in range(1, devices - 1, 2)] + [(g, g - 1) for g in range(2, devices, 2)],
    )
    before = lax.ppermute(normed, NODES, [(g, g + 2) for g in range(devices - 2)])
    after = lax.ppermute(normed, NODES, [(g + 2, g) for g in range(devices - 2)])

    extra = head_dim + 16
    query, sums, top = pl.pallas_call(
        near_kernel,
        out_shape=[
            jax.ShapeDtypeStruct((HEADS, LANES, nodes), bf16),
            jax.ShapeDtypeStruct((HEADS, extra, nodes), f32),
            jax.ShapeDtypeStruct((HEADS, 8, nodes), f32),
        ],
        in_specs=[VMEM] * 5 + [SMEM] * 2,
        out_specs=[VMEM] * 3,
        scratch_shapes=[
            pltpu.VMEM((width // LANES, 2 * nodes, LANES), bf16),
            pltpu.VMEM((HEADS, extra, 2 * nodes), bf16),
            pltpu.VMEM((2 * nodes, nodes), i32),
        ],
        compiler_params=params(32),
        cost_estimate=cost(8 << 30, 4 << 20),
        name="near",
    )(normed, side, w_query, w_key, w_value, order, window)

    return pl.pallas_call(
        far_kernel,
        out_shape=jax.ShapeDtypeStruct((nodes, width), bf16),
        in_specs=[VMEM] * 5 + [SMEM] * 2 + [VMEM] * 6 + [pl.BlockSpec(memory_space=pl.ANY)] * 2,
        out_specs=VMEM,
        scratch_shapes=[
            pltpu.VMEM((width // LANES, 3 * nodes, LANES), bf16),
            pltpu.VMEM((HEADS, extra, 3 * nodes), bf16),
            pltpu.VMEM((3 * nodes, nodes), i32),
            pltpu.VMEM((HEADS, head_dim, nodes), bf16),
            pltpu.VMEM(w_up.shape, bf16),
            pltpu.VMEM(w_down.shape, bf16),
            pltpu.SemaphoreType.DMA((2,)),
        ],
        compiler_params=params(40),
        cost_estimate=cost(8 << 30, 8 << 20),
        name="far",
    )(
        beyond, before, after, w_key, w_value, order, window,
        query, sums, top, state, w_out, gain_mlp.reshape(1, width), w_up, w_down,
    )


def solution(mesh):
    placed = (
        P(("groups", "band", "inner"), None),
        P(("groups", "band", "inner"), None),
        P(("groups", "band"), "inner", None, None, None),
        P(("groups", "band"), "inner", None, None, None),
        P(("groups", "band"), "inner", None, None),
        P(),
        P(),
        P(),
        P(),
        P("groups"),
        P(),
        P(),
        P(),
        P(),
    )
    return jax.shard_map(
        local,
        mesh=mesh,
        in_specs=placed,
        out_specs=P(("groups", "band", "inner"), None),
        check_vma=False,
    )
```

time: 216 us -> 90.9 us (0.42)
  the two profiles are of different devices: /device:TPU:15 before, /device:TPU:1 now
where the time goes in v1:
time: 90.9 us; the launch traced here: 90.4 us
  starting transfers between devices  29.2 us (32%)
  Pallas kernels  22.6 us (25%)
  blocking collectives  19.4 us (21%)
  waiting for transfers between devices  10.3 us (11%)
  local copies, waits for them, and re-layouts  8.15 us (9%)
    ppermute x11, starting transfers between devices, local(): lax.ppermute(block, NODES, route)  24 us
    all_gather x1, blocking collectives, local(): targets = lax.all_gather(targets, NODES, axis=0, tiled=True)  19.4 us
    pallas_call x1, Pallas kernels, local(): pl.pallas_call(far_kernel, out_shape=jax.ShapeDtypeStruct((nodes, width),...  11.1 us
    pallas_call x1, Pallas kernels, local(): pl.pallas_call(near_kernel, out_shape=[jax.ShapeDtypeStruct((HEADS, LANES...  8.23 us
    unnamed x28, local copies, waits for them, and re-layouts  5.17 us
    ppermute x1, waiting for transfers between devices, local(): lax.ppermute(normed, NODES, [(g, g + 2) for g in range(devices - 2)])  4.29 us
    ppermute x11, waiting for transfers between devices, local(): lax.ppermute(block, NODES, route)  4.25 us
    pallas_call x1, Pallas kernels, local(): pl.pallas_call(functools.partial(message_kernel, inners), out_shape=[jax....  2.37 us
  transfers between devices with their start and end apart: 15, of which 5 were waited for; matrix products, arithmetic and copies ran while one was open for 6% of the time, Pallas kernels for 9%

profile of v1, /device:TPU:1, one launch (start us, length us, event | category | flops | bytes accessed | tf_op | source)
XLA Modules:
  0.0 90.4 jit_solution(15854717365069682797)
XLA Ops:
  0.7 1.2 %copy-done.5 = bf16[1024,512]{1,0:T(8,128)(2,1)S(1)} copy-done((bf16[1024,512]{1,0:T(8,128)(2,1)S(1)}, bf16[1024,512]{1,0:T(8,128)(2,1)}, u32[]{:S(2)}) %copy-start.5) | copy-done | bytes 1048600
  1.9 1.0 %copy-done.6 = bf16[512,512]{1,0:T(8,128)(2,1)S(1)} copy-done((bf16[512,512]{1,0:T(8,128)(2,1)S(1)}, bf16[512,512]{1,0:T(8,128)(2,1)}, u32[]{:S(2)}) %copy-start.6) | copy-done | bytes 524312
  3.0 2.4 %messages.1 = (bf16[128,512]{1,0:T(8,128)(2,1)S(1)}, bf16[128,512]{1,0:T(8,128)(2,1)S(1)}, bf16[128,512]{1,0:T(8,128)(2,1)S(1)}, bf16[128,512]{1,0:T(8,128)(2,1)...) custom-call(bf16[1024,512]{1,0:T(8,128)(2,1)S(1)} %copy-done.5, ...), custom_call_target="tpu_custom_call" | custom-call | flops 2147483648 | bytes 4194304 | tf_op jit(solution)/shard_map/messages/pallas_call | solution.py:289
  5.4 1.3 %collective-permute-start = (bf16[128,512]{1,0:T(8,128)(2,1)S(1)}, bf16[128,512]{1,0:T(8,128)(2,1)S(1)}, u32[]{:S(2)}, u32[]{:S(2)}) collective-permute-start(bf16[128,512]{1,0:T(8,128)(2,1)S(1)} %get-tuple-element.22), channel_id=1, source_target_pairs={{4,0},{5,1},{6,2},{7,3},{8,4},{9,5},{10,6},{11,7},{12,8},{13,9},{1... | collective-permute-start | bytes 393224 | tf_op jit(solution)/shard_map/ppermute | solution.py:309
  6.7 1.3 %collective-permute-start.1 = (bf16[128,512]{1,0:T(8,128)(2,1)S(1)}, bf16[128,512]{1,0:T(8,128)(2,1)S(1)}, u32[]{:S(2)}, u32[]{:S(2)}) collective-permute-start(bf16[128,512]{1,0:T(8,128)(2,1)S(1)} %get-tuple-element.23), channel_id=1, source_target_pairs={{4,1},{5,0},{6,3},{7,2},{8,5},{9,4},{10,7},{11,6},{12,9},{13,8},{1... | collective-permute-start | bytes 393224 | tf_op jit(solution)/shard_map/ppermute | solution.py:309
  8.0 7.2 %collective-permute-start.10 = (bf16[128,512]{1,0:T(8,128)(2,1)S(1)}, bf16[128,512]{1,0:T(8,128)(2,1)S(1)}, u32[]{:S(2)}, u32[]{:S(2)}) collective-permute-start(bf16[128,512]{1,0:T(8,128)(2,1)S(1)} %get-tuple-element.33), channel_id=1, source_target_pairs={{0,7},{1,6},{2,5},{3,4},{4,11},{5,10},{6,9},{7,8},{8,15},{9,14},{1... | collective-permute-start | bytes 393224 | tf_op jit(solution)/shard_map/ppermute | solution.py:309
  15.2 1.3 %collective-permute-start.2 = (bf16[128,512]{1,0:T(8,128)(2,1)S(1)}, bf16[128,512]{1,0:T(8,128)(2,1)S(1)}, u32[]{:S(2)}, u32[]{:S(2)}) collective-permute-start(bf16[128,512]{1,0:T(8,128)(2,1)S(1)} %get-tuple-element.24), channel_id=1, source_target_pairs={{4,2},{5,3},{6,0},{7,1},{8,6},{9,7},{10,4},{11,5},{12,10},{13,11},... | collective-permute-start | bytes 393224 | tf_op jit(solution)/shard_map/ppermute | solution.py:309
  16.5 1.3 %collective-permute-start.3 = (bf16[128,512]{1,0:T(8,128)(2,1)S(1)}, bf16[128,512]{1,0:T(8,128)(2,1)S(1)}, u32[]{:S(2)}, u32[]{:S(2)}) collective-permute-start(bf16[128,512]{1,0:T(8,128)(2,1)S(1)} %get-tuple-element.25), channel_id=1, source_target_pairs={{4,3},{5,2},{6,1},{7,0},{8,7},{9,6},{10,5},{11,4},{12,11},{13,10},... | collective-permute-start | bytes 393224 | tf_op jit(solution)/shard_map/ppermute | solution.py:309
  18.2 1.9 %collective-permute-start.6 = (bf16[128,512]{1,0:T(8,128)(2,1)S(1)}, bf16[128,512]{1,0:T(8,128)(2,1)S(1)}, u32[]{:S(2)}, u32[]{:S(2)}) collective-permute-start(bf16[128,512]{1,0:T(8,128)(2,1)S(1)} %get-tuple-element.29), channel_id=1, source_target_pairs={{0,3},{1,2},{2,1},{3,0},{4,7},{5,6},{6,5},{7,4},{8,11},{9,10},{10,... | collective-permute-start | bytes 393224 | tf_op jit(solution)/shard_map/ppermute | solution.py:309
  20.1 3.4 %collective-permute-done.2.refs_2_ = bf16[128,512]{1,0:T(8,128)(2,1)S(1)} collective-permute-done((bf16[128,512]{1,0:T(8,128)(2,1)S(1)}, bf16[128,512]{1,0:T(8,128)(2,1)S(1)}, u32[]{:S(2)}, u32[]{:S(2)}) %collective-permute-start.2) | collective-permute-done | bytes 131104 | tf_op jit(solution)/shard_map/ppermute | solution.py:309
  23.5 2.1 %collective-permute-start.7 = (bf16[128,512]{1,0:T(8,128)(2,1)S(1)}, bf16[128,512]{1,0:T(8,128)(2,1)S(1)}, u32[]{:S(2)}, u32[]{:S(2)}) collective-permute-start(bf16[128,512]{1,0:T(8,128)(2,1)S(1)} %get-tuple-element.30), channel_id=1, source_target_pairs={{0,4},{1,5},{2,6},{3,7},{4,8},{5,9},{6,10},{7,11},{8,12},{9,13},{1... | collective-permute-start | bytes 393224 | tf_op jit(solution)/shard_map/ppermute | solution.py:309
  26.3 3.7 %collective-permute-start.8 = (bf16[128,512]{1,0:T(8,128)(2,1)S(1)}, bf16[128,512]{1,0:T(8,128)(2,1)S(1)}, u32[]{:S(2)}, u32[]{:S(2)}) collective-permute-start(bf16[128,512]{1,0:T(8,128)(2,1)S(1)} %get-tuple-element.31), channel_id=1, source_target_pairs={{0,5},{1,4},{2,7},{3,6},{4,9},{5,8},{6,11},{7,10},{8,13},{9,12},{1... | collective-permute-start | bytes 393224 | tf_op jit(solution)/shard_map/ppermute | solution.py:309
  30.1 3.8 %collective-permute-start.9 = (bf16[128,512]{1,0:T(8,128)(2,1)S(1)}, bf16[128,512]{1,0:T(8,128)(2,1)S(1)}, u32[]{:S(2)}, u32[]{:S(2)}) collective-permute-start(bf16[128,512]{1,0:T(8,128)(2,1)S(1)} %get-tuple-element.32), channel_id=1, source_target_pairs={{0,6},{1,7},{2,4},{3,5},{4,10},{5,11},{6,8},{7,9},{8,14},{9,15},{1... | collective-permute-start | bytes 393224 | tf_op jit(solution)/shard_map/ppermute | solution.py:309
  33.9 19.4 %all-gather = s32[16,12,128]{2,1,0:T(8,128)S(1)} all-gather(s32[1,12,128]{2,1,0:T(8,128)S(1)} %select_bitcast_fusion), channel_id=1, replica_groups=mesh['groups'=2,'band'=4,'inner'=4] {'band','inner'}, dimensions={0}, use_global_device_ids=true | all-gather | bytes 104448 | tf_op jit(solution)/shard_map/all_gather | solution.py:287
  53.4 2.7 %copy.24 = bf16[512,1536]{0,1:T(8,128)(2,1)} copy(bf16[512,1536]{1,0:T(8,128)(2,1)} %param.22) | data formatting | bytes 3145728 | tf_op args[8]
  56.2 1.0 %merge.1 = (f32[256,512]{1,0:T(8,128)S(1)}, bf16[256,512]{1,0:T(8,128)(2,1)S(1)}) custom-call(bf16[128,512]{1,0:T(8,128)(2,1)S(1)} %collective-permute-done.refs_0_, bf16[128,512]{1,0:T(8,128)(2,1)S(1)} %collective-permute-done.1.refs_1_, bf16[128,512]{1,0:T(8,128)(2,1)S(1)} %collective-permute-done.2.refs_2_, ...), custom_call_target="tpu_custom_call" | custom-call | flops 536870912 | bytes 4194304 | tf_op jit(solution)/shard_map/merge/pallas_call | solution.py:323
  58.4 1.3 %copy.26.wk_ref = bf16[512,512]{1,0:T(8,128)(2,1)S(1)} copy(bf16[512,512]{0,1:T(8,128)(2,1)} %bitcast.18) | data formatting | bytes 1048576 | tf_op jit(solution)/shard_map/reshape;squeeze | solution.py:313
  60.0 1.9 %collective-permute-start.11 = (bf16[256,512]{1,0:T(8,128)(2,1)S(1)}, bf16[256,512]{1,0:T(8,128)(2,1)S(1)}, u32[]{:S(2)}, u32[]{:S(2)}) collective-permute-start(bf16[256,512]{1,0:T(8,128)(2,1)S(1)} %get-tuple-element.34.own_ref), channel_id=1, source_target_pairs={{1,2},{3,4},{5,6},{7,8},{9,10},{11,12},{13,14},{2,1},{4,3},{6,5},{... | collective-permute-start | bytes 786440 | tf_op jit(solution)/shard_map/ppermute | solution.py:337
  61.9 1.7 %collective-permute-start.12 = (bf16[256,512]{1,0:T(8,128)(2,1)S(1)}, bf16[256,512]{1,0:T(8,128)(2,1)S(1)}, u32[]{:S(2)}, u32[]{:S(2)}) collective-permute-start(bf16[256,512]{1,0:T(8,128)(2,1)S(1)} %get-tuple-element.34.own_ref), channel_id=1, source_target_pairs={{0,2},{1,3},{2,4},{3,5},{4,6},{5,7},{6,8},{7,9},{8,10},{9,11},{10,... | collective-permute-start | bytes 786440 | tf_op jit(solution)/shard_map/ppermute | solution.py:342
  63.6 1.3 %collective-permute-start.13 = (bf16[256,512]{1,0:T(8,128)(2,1)S(1)}, bf16[256,512]{1,0:T(8,128)(2,1)S(1)}, u32[]{:S(2)}, u32[]{:S(2)}) collective-permute-start(bf16[256,512]{1,0:T(8,128)(2,1)S(1)} %get-tuple-element.34.own_ref), channel_id=1, source_target_pairs={{2,0},{3,1},{4,2},{5,3},{6,4},{7,5},{8,6},{9,7},{10,8},{11,9},{12,... | collective-permute-start | bytes 786440 | tf_op jit(solution)/shard_map/ppermute | solution.py:343
  65.0 8.2 %near.1 = (bf16[16,128,256]{2,1,0:T(8,128)(2,1)S(1)}, f32[16,48,256]{2,1,0:T(8,128)S(1)}, f32[16,8,256]{2,1,0:T(8,128)S(1)}) custom-call(bf16[256,512]{1,0:T(8,128)(2,1)S(1)} %get-tuple-element.34.own_ref, bf16[256,512]{1,0:T(8,128)(2,1)S(1)} %collective-permute-done.14.side_ref, bf16[512,512]{1,0:T(8,128)(2,1)S(1)} %bitcast.14, ...), custom_call_target="tpu_custom_call" | custom-call | flops 8589934592 | bytes 4194304 | tf_op jit(solution)/shard_map/near/pallas_call | solution.py:346
  73.2 1.8 %collective-permute-done.11.beyond_ref = bf16[256,512]{1,0:T(8,128)(2,1)S(1)} collective-permute-done((bf16[256,512]{1,0:T(8,128)(2,1)S(1)}, bf16[256,512]{1,0:T(8,128)(2,1)S(1)}, u32[]{:S(2)}, u32[]{:S(2)}) %collective-permute-start.11) | collective-permute-done | bytes 262176 | tf_op jit(solution)/shard_map/ppermute | solution.py:337
  75.0 4.3 %collective-permute-done.12.before_ref = bf16[256,512]{1,0:T(8,128)(2,1)S(1)} collective-permute-done((bf16[256,512]{1,0:T(8,128)(2,1)S(1)}, bf16[256,512]{1,0:T(8,128)(2,1)S(1)}, u32[]{:S(2)}, u32[]{:S(2)}) %collective-permute-start.12) | collective-permute-done | bytes 262176 | tf_op jit(solution)/shard_map/ppermute | solution.py:342
  79.3 11.1 %far.1 = bf16[256,512]{1,0:T(8,128)(2,1)} custom-call(bf16[256,512]{1,0:T(8,128)(2,1)S(1)} %collective-permute-done.11.beyond_ref, bf16[256,512]{1,0:T(8,128)(2,1)S(1)} %collective-permute-done.12.before_ref, bf16[256,512]{1,0:T(8,128)(2,1)S(1)} %collective-permute-done.13.after_ref, bf16[512,512]{1,0:T(8,128)(2,1)S(1)} %copy.26.wk_ref, ...), custom_call_target="tpu_custom_call" | custom-call | flops 8589934592 | bytes 8388608 | tf_op jit(solution)/shard_map/far/pallas_call | solution.py:365
  (48 shorter events, 3.5 us)
Async XLA Ops:
  3.0 14.9 %copy-start.11 = (s32[1,1,3,4,128]{4,3,2,1,0:T(4,128)S(1)}, s32[1,1,3,4,128]{4,3,2,1,0:T(4,128)}, u32[]{:S(2)}) copy-start(s32[1,1,3,4,128]{4,3,2,1,0:T(4,128)} %param.17) | copy-start | bytes 18436
  3.0 14.9 %copy-start.12 = (s32[1,1,3,4]{3,1,2,0:T(1,128)S(1)}, s32[1,1,3,4]{3,1,2,0:T(1,128)}, u32[]{:S(2)}) copy-start(s32[1,1,3,4]{3,1,2,0:T(1,128)} %param.18) | copy-start | bytes 148
  5.4 12.4 %collective-permute-start = (bf16[128,512]{1,0:T(8,128)(2,1)S(1)}, bf16[128,512]{1,0:T(8,128)(2,1)S(1)}, u32[]{:S(2)}, u32[]{:S(2)}) collective-permute-start(bf16[128,512]{1,0:T(8,128)(2,1)S(1)} %get-tuple-element.22), channel_id=1, source_target_pairs={{4,0},{5,1},{6,2},{7,3},{8,4},{9,5},{10,6},{11,7},{12,8},{13,9},{1... | collective-permute-start | bytes 393224 | tf_op jit(solution)/shard_map/ppermute | solution.py:309
  6.7 11.4 %collective-permute-start.1 = (bf16[128,512]{1,0:T(8,128)(2,1)S(1)}, bf16[128,512]{1,0:T(8,128)(2,1)S(1)}, u32[]{:S(2)}, u32[]{:S(2)}) collective-permute-start(bf16[128,512]{1,0:T(8,128)(2,1)S(1)} %get-tuple-element.23), channel_id=1, source_target_pairs={{4,1},{5,0},{6,3},{7,2},{8,5},{9,4},{10,7},{11,6},{12,9},{13,8},{1... | collective-permute-start | bytes 393224 | tf_op jit(solution)/shard_map/ppermute | solution.py:309
  8.0 10.2 %collective-permute-start.10 = (bf16[128,512]{1,0:T(8,128)(2,1)S(1)}, bf16[128,512]{1,0:T(8,128)(2,1)S(1)}, u32[]{:S(2)}, u32[]{:S(2)}) collective-permute-start(bf16[128,512]{1,0:T(8,128)(2,1)S(1)} %get-tuple-element.33), channel_id=1, source_target_pairs={{0,7},{1,6},{2,5},{3,4},{4,11},{5,10},{6,9},{7,8},{8,15},{9,14},{1... | collective-permute-start | bytes 393224 | tf_op jit(solution)/shard_map/ppermute | solution.py:309
  15.2 8.3 %collective-permute-start.2 = (bf16[128,512]{1,0:T(8,128)(2,1)S(1)}, bf16[128,512]{1,0:T(8,128)(2,1)S(1)}, u32[]{:S(2)}, u32[]{:S(2)}) collective-permute-start(bf16[128,512]{1,0:T(8,128)(2,1)S(1)} %get-tuple-element.24), channel_id=1, source_target_pairs={{4,2},{5,3},{6,0},{7,1},{8,6},{9,7},{10,4},{11,5},{12,10},{13,11},... | collective-permute-start | bytes 393224 | tf_op jit(solution)/shard_map/ppermute | solution.py:309
  16.5 9.9 %collective-permute-start.3 = (bf16[128,512]{1,0:T(8,128)(2,1)S(1)}, bf16[128,512]{1,0:T(8,128)(2,1)S(1)}, u32[]{:S(2)}, u32[]{:S(2)}) collective-permute-start(bf16[128,512]{1,0:T(8,128)(2,1)S(1)} %get-tuple-element.25), channel_id=1, source_target_pairs={{4,3},{5,2},{6,1},{7,0},{8,7},{9,6},{10,5},{11,4},{12,11},{13,10},... | collective-permute-start | bytes 393224 | tf_op jit(solution)/shard_map/ppermute | solution.py:309
  17.8 12.3 %collective-permute-start.4 = (bf16[128,512]{1,0:T(8,128)(2,1)S(1)}, bf16[128,512]{1,0:T(8,128)(2,1)S(1)}, u32[]{:S(2)}, u32[]{:S(2)}) collective-permute-start(bf16[128,512]{1,0:T(8,128)(2,1)S(1)} %get-tuple-element.27), channel_id=1, source_target_pairs={{0,1},{1,0},{2,3},{3,2},{4,5},{5,4},{6,7},{7,6},{8,9},{9,8},{10,11... | collective-permute-start | bytes 393224 | tf_op jit(solution)/shard_map/ppermute | solution.py:309
  18.0 38.1 %collective-permute-start.5 = (bf16[128,512]{1,0:T(8,128)(2,1)S(1)}, bf16[128,512]{1,0:T(8,128)(2,1)S(1)}, u32[]{:S(2)}, u32[]{:S(2)}) collective-permute-start(bf16[128,512]{1,0:T(8,128)(2,1)S(1)} %get-tuple-element.28), channel_id=1, source_target_pairs={{0,2},{1,3},{2,0},{3,1},{4,6},{5,7},{6,4},{7,5},{8,10},{9,11},{10,... | collective-permute-start | bytes 393224 | tf_op jit(solution)/shard_map/ppermute | solution.py:309
  18.2 37.9 %collective-permute-start.6 = (bf16[128,512]{1,0:T(8,128)(2,1)S(1)}, bf16[128,512]{1,0:T(8,128)(2,1)S(1)}, u32[]{:S(2)}, u32[]{:S(2)}) collective-permute-start(bf16[128,512]{1,0:T(8,128)(2,1)S(1)} %get-tuple-element.29), channel_id=1, source_target_pairs={{0,3},{1,2},{2,1},{3,0},{4,7},{5,6},{6,5},{7,4},{8,11},{9,10},{10,... | collective-permute-start | bytes 393224 | tf_op jit(solution)/shard_map/ppermute | solution.py:309
  23.5 32.6 %collective-permute-start.7 = (bf16[128,512]{1,0:T(8,128)(2,1)S(1)}, bf16[128,512]{1,0:T(8,128)(2,1)S(1)}, u32[]{:S(2)}, u32[]{:S(2)}) collective-permute-start(bf16[128,512]{1,0:T(8,128)(2,1)S(1)} %get-tuple-element.30), channel_id=1, source_target_pairs={{0,4},{1,5},{2,6},{3,7},{4,8},{5,9},{6,10},{7,11},{8,12},{9,13},{1... | collective-permute-start | bytes 393224 | tf_op jit(solution)/shard_map/ppermute | solution.py:309
  26.3 29.8 %collective-permute-start.8 = (bf16[128,512]{1,0:T(8,128)(2,1)S(1)}, bf16[128,512]{1,0:T(8,128)(2,1)S(1)}, u32[]{:S(2)}, u32[]{:S(2)}) collective-permute-start(bf16[128,512]{1,0:T(8,128)(2,1)S(1)} %get-tuple-element.31), channel_id=1, source_target_pairs={{0,5},{1,4},{2,7},{3,6},{4,9},{5,8},{6,11},{7,10},{8,13},{9,12},{1... | collective-permute-start | bytes 393224 | tf_op jit(solution)/shard_map/ppermute | solution.py:309
  30.1 26.0 %collective-permute-start.9 = (bf16[128,512]{1,0:T(8,128)(2,1)S(1)}, bf16[128,512]{1,0:T(8,128)(2,1)S(1)}, u32[]{:S(2)}, u32[]{:S(2)}) collective-permute-start(bf16[128,512]{1,0:T(8,128)(2,1)S(1)} %get-tuple-element.32), channel_id=1, source_target_pairs={{0,6},{1,7},{2,4},{3,5},{4,10},{5,11},{6,8},{7,9},{8,14},{9,15},{1... | collective-permute-start | bytes 393224 | tf_op jit(solution)/shard_map/ppermute | solution.py:309
  53.4 2.8 %copy-start = (bf16[512,512]{1,0:T(8,128)(2,1)S(1)}, bf16[512,512]{1,0:T(8,128)(2,1)}, u32[]{:S(2)}) copy-start(bf16[512,512]{1,0:T(8,128)(2,1)} %refs_14_.1) | copy-start | bytes 1572868
  53.4 2.8 %copy-start.1 = (bf16[256,512]{1,0:T(8,128)(2,1)S(1)}, bf16[256,512]{1,0:T(8,128)(2,1)}, u32[]{:S(2)}) copy-start(bf16[256,512]{1,0:T(8,128)(2,1)} %refs_13_.1) | copy-start | bytes 786436
  53.4 2.8 %copy-start.2 = (f32[512]{0:T(512)S(1)}, f32[512]{0:T(512)}, u32[]{:S(2)}) copy-start(f32[512]{0:T(512)} %param.21) | copy-start | bytes 6148
  57.1 7.8 %collective-permute-start.14 = (bf16[256,512]{1,0:T(8,128)(2,1)S(1)}, bf16[256,512]{1,0:T(8,128)(2,1)S(1)}, u32[]{:S(2)}, u32[]{:S(2)}) collective-permute-start(bf16[256,512]{1,0:T(8,128)(2,1)S(1)} %get-tuple-element.34.own_ref), channel_id=1, source_target_pairs={{0,1},{1,0},{2,3},{3,2},{4,5},{5,4},{6,7},{7,6},{8,9},{9,8},{10,11... | collective-permute-start | bytes 786440 | tf_op jit(solution)/shard_map/ppermute | solution.py:336
  60.0 15.0 %collective-permute-start.11 = (bf16[256,512]{1,0:T(8,128)(2,1)S(1)}, bf16[256,512]{1,0:T(8,128)(2,1)S(1)}, u32[]{:S(2)}, u32[]{:S(2)}) collective-permute-start(bf16[256,512]{1,0:T(8,128)(2,1)S(1)} %get-tuple-element.34.own_ref), channel_id=1, source_target_pairs={{1,2},{3,4},{5,6},{7,8},{9,10},{11,12},{13,14},{2,1},{4,3},{6,5},{... | collective-permute-start | bytes 786440 | tf_op jit(solution)/shard_map/ppermute | solution.py:337
  61.9 17.3 %collective-permute-start.12 = (bf16[256,512]{1,0:T(8,128)(2,1)S(1)}, bf16[256,512]{1,0:T(8,128)(2,1)S(1)}, u32[]{:S(2)}, u32[]{:S(2)}) collective-permute-start(bf16[256,512]{1,0:T(8,128)(2,1)S(1)} %get-tuple-element.34.own_ref), channel_id=1, source_target_pairs={{0,2},{1,3},{2,4},{3,5},{4,6},{5,7},{6,8},{7,9},{8,10},{9,11},{10,... | collective-permute-start | bytes 786440 | tf_op jit(solution)/shard_map/ppermute | solution.py:342
  63.6 15.6 %collective-permute-start.13 = (bf16[256,512]{1,0:T(8,128)(2,1)S(1)}, bf16[256,512]{1,0:T(8,128)(2,1)S(1)}, u32[]{:S(2)}, u32[]{:S(2)}) collective-permute-start(bf16[256,512]{1,0:T(8,128)(2,1)S(1)} %get-tuple-element.34.own_ref), channel_id=1, source_target_pairs={{2,0},{3,1},{4,2},{5,3},{6,4},{7,5},{8,6},{9,7},{10,8},{11,9},{12,... | collective-permute-start | bytes 786440 | tf_op jit(solution)/shard_map/ppermute | solution.py:343
  64.9 14.3 %copy-start.3 = (bf16[512,2048]{1,0:T(8,128)(2,1)S(1)}, bf16[512,2048]{1,0:T(8,128)(2,1)}, u32[]{:S(2)}) copy-start(bf16[512,2048]{1,0:T(8,128)(2,1)} %up_ref.1) | copy-start | bytes 6291460
  65.0 14.3 %copy-start.4 = (bf16[2048,512]{1,0:T(8,128)(2,1)S(1)}, bf16[2048,512]{1,0:T(8,128)(2,1)}, u32[]{:S(2)}) copy-start(bf16[2048,512]{1,0:T(8,128)(2,1)} %down_ref.1) | copy-start | bytes 6291460
  65.0 14.3 %copy-start.7 = (bf16[512,512]{1,0:T(8,128)(2,1)S(1)}, bf16[512,512]{1,0:T(8,128)(2,1)}, u32[]{:S(2)}) copy-start(bf16[512,512]{1,0:T(8,128)(2,1)} %w_out_ref.1) | copy-start | bytes 1572868
  65.0 14.3 %copy-start.8 = (f32[512]{0:T(512)S(1)}, f32[512]{0:T(512)}, u32[]{:S(2)}) copy-start(f32[512]{0:T(512)} %param.25) | copy-start | bytes 6148
  (4 other events, 5.9 us)
